TPU v7x, 32 devices: a whole 2x2x4 slice. The times are simulated.
32 devices in a mesh: dp: 4 (over y, core), tensor: 8 (over z, x).
Axes of the slice: x: 2, y: 2, z: 4, core: 2. Of those that a mesh axis runs over, the one named last changes fastest.
Arguments:
- layer_input: bfloat16 [4096, 8192], P('dp', 'tensor'), may hold values from -6 to 6
- output_grad: bfloat16 [4096, 1024], P(('dp', 'tensor')), may hold values from -6 to 6
- key_weight: bfloat16 [8192, 1024], P('tensor'), may hold values from -0.0625 to 0.0625
- adapter_down: bfloat16 [128, 16, 8192], P('dp', None, 'tensor'), may hold values from -0.0625 to 0.0625
- adapter_up: bfloat16 [128, 16, 1024], P('dp', None, 'tensor'), may hold values from -0.1875 to 0.1875
- segment_adapter: int32 [32], replicated, may hold values from 0 to 127
- adapter_slot: int32 [128], replicated, may hold values from 0 to 127, each once
- live_segments: int32 [4], P('dp'), may hold values from 1 to 8, as said below
Outputs:
- input_grad: bfloat16 [4096, 8192], P('dp', 'tensor')
- down_grad: bfloat16 [128, 16, 8192], P('dp', None, 'tensor')
- up_grad: bfloat16 [128, 16, 1024], P('dp', None, 'tensor')
Inputs may be any that keep to these rules, and one draw needn't show every extreme that they name: `live_segments`: some data group has all 8 segments live; a group's segments at or past its count are padding.
All inputs are finite; a program needn't handle non-finite values.
Results may differ from a plain program's by a relative error of at most 0.0057.
Values may be sent and summed in bfloat16 or wider, within the bound.
A program may use at most 64 MiB of HBM per device.

v0:
```python
import functools

import jax
import jax.numpy as jnp
from jax import lax
from jax.experimental import pallas as pl
from jax.experimental.pallas import tpu as pltpu
from jax.sharding import PartitionSpec as P

MESH = pl.DeviceIdType.MESH
CHUNKS = 4
VMEM_LIMIT = 62 * 1024 * 1024
NT = (((1,), (1,)), ((), ()))
TN = (((0,), (0,)), ((), ()))


def fused_kernel(
    dims,
    adapter_hbm, slot_hbm, live_hbm,
    x_hbm, og_hbm, kw_hbm, ad_hbm, au_hbm,
    ig_hbm, dg_hbm, ug_hbm,
    adapter_s, slot_s, live_s, seg_slot, first,
    x_v, kw_v, ad_v, au_v, og_v, whole, ig_v, dg_v, ug_v,
    s1d_out, s1d_in, s2d_out, s2d_in, fu_out, fu_in,
    down_seg, up_seg, up_own, lr, pr_out, pr_in, su_out, su_in, rows_d, rows_u,
    load_sem, store_sem, blk_send, blk_recv, s1_send, s1_recv, s2_send, s2_recv, fu_send, fu_recv,
    up_send, up_recv, lr_send, lr_recv, pr_send, pr_recv, su_send, su_recv,
    rwy_send, rwu_send, rwc_send, rw_recv,
):
    T, X, Q, S, L, R, W, K, KS, PO = dims
    Z, Y = T // X, Q // 2
    half = L // CHUNKS
    t, q = lax.axis_index("tensor"), lax.axis_index("dp")
    z, x = t // X, lax.rem(t, X)
    y, c = q // 2, lax.rem(q, 2)
    mate = q + 1 - 2 * c
    pending = []

    def send(src, dst, send_sem, recv_sem, to, when=None):
        copy = pltpu.make_async_remote_copy(
            src_ref=src, dst_ref=dst, send_sem=send_sem, recv_sem=recv_sem,
            device_id=to, device_id_type=MESH,
        )
        if when is None:
            copy.start()
        else:
            pl.when(when)(copy.start)
        pending.append((when, copy))

    def arrived(ref, sem, when=None):
        copy = pltpu.make_async_copy(ref, ref, sem)
        if when is None:
            copy.wait()
        else:
            pl.when(when)(copy.wait)

    scalars = [
        pltpu.make_async_copy(adapter_hbm, adapter_s, load_sem.at[5]),
        pltpu.make_async_copy(slot_hbm, slot_s, load_sem.at[6]),
        pltpu.make_async_copy(live_hbm, live_s, load_sem.at[7]),
    ]
    loads = [
        pltpu.make_async_copy(og_hbm, og_v, load_sem.at[0]),
        pltpu.make_async_copy(au_hbm, au_v, load_sem.at[2]),
        pltpu.make_async_copy(ad_hbm, ad_v, load_sem.at[1]),
    ]
    later_loads = [
        pltpu.make_async_copy(x_hbm, x_v, load_sem.at[3]),
        pltpu.make_async_copy(kw_hbm, kw_v, load_sem.at[4]),
    ]
    for copy in scalars + loads:
        copy.start()

    tensor_peers = [lax.rem(t + j, T) for j in range(1, T)]
    far = [lax.rem(y + j, Y) for j in range(1, Y)]
    barrier = pltpu.get_barrier_semaphore()
    for peer in tensor_peers:
        pl.semaphore_signal(barrier, inc=1, device_id={"tensor": peer}, device_id_type=MESH)
    dp_peers = [lax.rem(q + j, Q) for j in range(1, Q)]
    for peer in dp_peers:
        pl.semaphore_signal(barrier, inc=1, device_id={"dp": peer}, device_id_type=MESH)

    scalars[2].wait()
    loads[0].wait()
    live = t < live_s[0]
    own_rows = jnp.where(live, og_v[...], jnp.zeros((L, K), jnp.bfloat16))
    whole[t] = own_rows

    pl.semaphore_wait(barrier, T - 1 + Q - 1)

    def rows_of(origin, part):
        return whole.at[origin, pl.ds(part * half, half)]

    def to_z(origin, part, up, when):
        step = 1 if up else -1
        edge = (z + 1 < Z) if up else (z > 0)
        when = edge if when is None else jnp.logical_and(when, edge)
        ref = rows_of(origin, part)
        send(ref, ref, blk_send.at[origin, part, 0 if up else 1], blk_recv.at[origin, part],
             {"tensor": t + step * X}, when)

    def to_x(origin, part, when):
        ref = rows_of(origin, part)
        for j in range(1, X):
            to = z * X + lax.rem(x + j, X)
            send(ref, ref, blk_send.at[origin, part, 1 + j], blk_recv.at[origin, part],
                 {"tensor": to}, when)

    paired = X == 2 and Z % 2 == 0
    direct = CHUNKS // 2 if paired else CHUNKS
    pair_z = z + 1 - 2 * lax.rem(z, 2)
    column = z * X + lax.rem(x + 1, X)
    for part in range(CHUNKS):
        to_z(t, part, True, None)
        to_z(t, part, False, None)
        to_x(t, part, None)

    def forward(step, part):
        for sign in (-1, 1):
            row = z + sign * step
            inside = jnp.logical_and(row >= 0, row < Z)
            origin = jnp.where(inside, row, z) * X + x
            arrived(rows_of(origin, part), blk_recv.at[origin, part], inside)
            to_z(origin, part, sign < 0, inside)
            across = inside
            if part >= direct:
                across = jnp.logical_and(inside, row != pair_z)
            to_x(origin, part, across)

    def share(part):
        if paired:
            ref = rows_of(column, part)
            arrived(ref, blk_recv.at[column, part])
            send(ref, ref, blk_send.at[column, part, 0], blk_recv.at[column, part],
                 {"tensor": pair_z * X + x})

    for copy in scalars[:2]:
        copy.wait()
    for s in range(Q * S):
        seg_slot[s] = slot_s[adapter_s[s]]

    def owned(index):
        local = seg_slot[index] - q * PO
        inside = jnp.logical_and(local >= 0, local < PO)
        return inside, jnp.clip(local, 0, PO - 1)

    loads[1].wait()

    def choose_up(i, carry):
        group, s = i // S, lax.rem(i, S)
        inside, local = owned(i)
        fu_out[group, s] = jnp.where(inside, au_v[local], jnp.zeros((R, KS), jnp.bfloat16))
        return carry

    lax.fori_loop(0, Q * S, choose_up, 0)
    for peer in dp_peers:
        send(fu_out.at[peer], fu_in.at[q], fu_send.at[peer], fu_recv.at[q], {"dp": peer})

    loads[2].wait()

    def choose_down(i, carry):
        group, s = i // S, lax.rem(i, S)
        inside, local = owned((group * 2 + 1 - c) * S + s)
        s1d_out[group, s] = jnp.where(inside, ad_v[local], jnp.zeros((R, W), jnp.bfloat16))
        return carry

    lax.fori_loop(0, Y * S, choose_down, 0)
    for copy in later_loads:
        copy.start()
    send(s1d_out, s1d_in, s1_send.at[0], s1_recv.at[0], {"dp": mate})

    def first_of(p, carry):
        slot = q * PO + p
        for group in range(Q):
            index = jnp.int32(-1)
            for s in reversed(range(S)):
                index = jnp.where(seg_slot[group * S + s] == slot, jnp.int32(s), index)
            first[p * Q + group] = index
        return carry

    lax.fori_loop(0, PO, first_of, 0)

    def combine_down(i, carry):
        group, s = i // S, lax.rem(i, S)
        inside, local = owned((group * 2 + c) * S + s)
        s2d_out[group, s] = jnp.where(inside, ad_v[local], s1d_in[group, s])
        return carry

    arrived(s1d_in, s1_recv.at[0])
    lax.fori_loop(0, Y * S, combine_down, 0)
    for other in far:
        send(s2d_out.at[other], s2d_in.at[y], s2_send.at[other, 0], s2_recv.at[y, 0],
             {"dp": other * 2 + c})

    forward(1, 0)

    total = fu_out[q]
    for peer in dp_peers:
        arrived(fu_in.at[peer], fu_recv.at[peer])
        total = total + fu_in[peer]
    up_seg[...] = total
    for peer in tensor_peers:
        send(up_seg.at[peer], up_own.at[t], up_send.at[peer], up_recv.at[t], {"tensor": peer})
    up_own[t] = up_seg[t]

    forward(1, 1)
    forward(1, 2)

    for peer in tensor_peers:
        arrived(up_own.at[peer], up_recv.at[peer])
    acc = jnp.zeros((R, L), jnp.float32)
    for p in range(T):
        acc = acc + lax.dot_general(
            up_own[p], whole[t, :, p * KS:(p + 1) * KS], NT, preferred_element_type=jnp.float32
        )
    lr[t] = acc.astype(jnp.bfloat16)
    for peer in tensor_peers:
        send(lr.at[t], lr.at[t], lr_send.at[peer], lr_recv.at[t], {"tensor": peer})

    share(2)
    forward(1, 3)
    share(3)
    if Z > 2:
        forward(2, 0)

    for other in far:
        arrived(s2d_in.at[other], s2_recv.at[other, 0])
    later_loads[0].wait()

    def down_of(s, carry):
        rows = s2d_out[y, s]
        for other in far:
            rows = rows + s2d_in[other, s]
        down_seg[s] = rows
        pr_out[s] = lax.dot_general(rows, x_v[s], NT, preferred_element_type=jnp.float32)
        return carry

    lax.fori_loop(0, S, down_of, 0)
    for peer in tensor_peers:
        send(pr_out.at[peer], pr_in.at[t], pr_send.at[peer], pr_recv.at[t], {"tensor": peer})
    pr_in[t] = pr_out[t]

    if Z > 2:
        forward(2, 1)

    for peer in tensor_peers:
        arrived(lr.at[peer], lr_recv.at[peer])

    own_slots = [seg_slot[q * S + s] for s in range(S)]

    def merged(parts, u, zero):
        return [jnp.where(own_slots[u] == own_slots[s], parts[s], zero) for s in range(S)]

    zero_l = jnp.zeros((R, L), jnp.bfloat16)
    ranks = [lr[s] for s in range(S)]
    left = jnp.concatenate(
        [jnp.concatenate(merged(ranks, u, zero_l), axis=1) for u in range(S)], axis=0
    )
    tile = 256
    for n in range(W // tile):
        columns = slice(n * tile, (n + 1) * tile)
        right = jnp.concatenate([x_v[s, :, columns] for s in range(S)], axis=0)
        grad = 2.0 * jnp.dot(left, right, preferred_element_type=jnp.float32)
        rows_d[q, :, :, columns] = grad.astype(jnp.bfloat16).reshape(S, R, tile)
    for other in far:
        send(rows_d.at[q], rows_d.at[q], rwy_send.at[other], rw_recv.at[q, 0],
             {"dp": other * 2 + c})
    send(rows_d.at[q], rows_d.at[q], rwc_send.at[q], rw_recv.at[q, 0], {"dp": mate})

    if Z > 2:
        forward(2, 2)

    later_loads[1].wait()

    def block_row(row):
        left_rows = whole[pl.ds(row * X, X)].reshape(X * L, K)
        for n in range(W // tile):
            at = slice(n * tile, (n + 1) * tile)
            value = lax.dot_general(left_rows, kw_v[at, :], NT, preferred_element_type=jnp.float32)
            for j in range(X):
                origin = row * X + j
                extra = lax.dot_general(
                    lr[origin], down_seg[origin, :, at], TN, preferred_element_type=jnp.float32
                )
                ig_v[origin, :, at] = (value[j * L:(j + 1) * L] + 2.0 * extra).astype(jnp.bfloat16)
        rows = pl.ds(row * X, X)
        pltpu.make_async_copy(ig_v.at[rows], ig_hbm.at[rows], store_sem.at[row]).start()

    def wait_side(row, parts):
        for j in range(1, X):
            origin = row * X + lax.rem(x + j, X)
            for part in parts:
                arrived(rows_of(origin, part), blk_recv.at[origin, part])

    def nearest(i):
        low, high = z, Z - 1 - z
        both = jnp.minimum(low, high)
        near = z + (-1 if i % 2 else 1) * ((i + 1) // 2)
        beyond = jnp.where(low < high, z + (i - both), z - (i - both))
        return jnp.where(i <= 2 * both, near, beyond)

    wait_side(z, range(direct))
    block_row(z)
    if Z > 2:
        forward(2, 3)

    for peer in tensor_peers:
        arrived(pr_in.at[peer], pr_recv.at[peer])
    acc = pr_in[0]
    for p in range(1, T):
        acc = acc + pr_in[p]
    projected = acc.astype(jnp.bfloat16)
    for p in range(T):
        su_out[p] = 2.0 * jnp.dot(
            projected, whole[t, :, p * KS:(p + 1) * KS], preferred_element_type=jnp.float32
        )
    for peer in tensor_peers:
        send(su_out.at[peer], su_in.at[t], su_send.at[peer], su_recv.at[t], {"tensor": peer})
    su_in[t] = su_out[t]

    for step in range(3, Z):
        forward(step, 0)
    wait_side(nearest(1), range(CHUNKS))
    block_row(nearest(1))
    for step in range(3, Z):
        forward(step, 1)

    for peer in tensor_peers:
        arrived(su_in.at[peer], su_recv.at[peer])
    zero_u = jnp.zeros((R, KS), jnp.float32)
    for u in range(S):
        total = zero_u
        for s in range(S):
            total = total + jnp.where(own_slots[u] == own_slots[s], su_in[s], zero_u)
        rows_u[q, u] = total.astype(jnp.bfloat16)
    for peer in dp_peers:
        send(rows_u.at[q], rows_u.at[q], rwu_send.at[peer], rw_recv.at[q, 1], {"dp": peer})

    for i in range(2, Z - 1):
        wait_side(nearest(i), range(CHUNKS))
        block_row(nearest(i))
    for step in range(3, Z):
        forward(step, 2)
    for other in far:
        origin = other * 2 + c
        arrived(rows_d.at[origin], rw_recv.at[origin, 0])
        send(rows_d.at[origin], rows_d.at[origin], rwc_send.at[origin],
             rw_recv.at[origin, 0], {"dp": mate})
    for step in range(3, Z):
        forward(step, 3)

    for group in range(Y):
        origin = group * 2 + 1 - c
        arrived(rows_d.at[origin], rw_recv.at[origin, 0])
    for peer in dp_peers:
        arrived(rows_u.at[peer], rw_recv.at[peer, 1])

    def owner_rows(p, carry):
        down_total = jnp.zeros((R, W), jnp.float32)
        up_total = jnp.zeros((R, KS), jnp.float32)
        for group in range(Q):
            index = first[p * Q + group]
            has = index >= 0
            index = jnp.maximum(index, 0)
            down_total += jnp.where(has, rows_d[group, index].astype(jnp.float32), 0.0)
            up_total += jnp.where(has, rows_u[group, index].astype(jnp.float32), 0.0)
        dg_v[p] = down_total.astype(jnp.bfloat16)
        ug_v[p] = up_total.astype(jnp.bfloat16)
        return carry

    lax.fori_loop(0, PO, owner_rows, 0, unroll=2)
    stores = [
        pltpu.make_async_copy(dg_v, dg_hbm, store_sem.at[Z]),
        pltpu.make_async_copy(ug_v, ug_hbm, store_sem.at[Z + 1]),
    ]
    for copy in stores:
        copy.start()

    if Z > 2:
        wait_side(nearest(Z - 1), range(CHUNKS))
        block_row(nearest(Z - 1))

    for when, copy in pending:
        if when is None:
            copy.wait_send()
        else:
            pl.when(when)(copy.wait_send)
    for row in range(Z):
        rows = pl.ds(row * X, X)
        pltpu.make_async_copy(ig_v.at[rows], ig_hbm.at[rows], store_sem.at[row]).wait()
    for copy in stores:
        copy.wait()


def store_kernel(a, b, c, a_out, b_out, c_out, sem):
    copies = [pltpu.make_async_copy(c, c_out, sem.at[0])]
    for src, dst, pieces in ((a, a_out, 4), (b, b_out, 2)):
        count = src.shape[0] // pieces
        for i in range(pieces):
            at = pl.ds(i * count, count)
            copies.append(pltpu.make_async_copy(src.at[at], dst.at[at], sem.at[len(copies)]))
    for copy in copies:
        copy.start()
    for copy in copies:
        copy.wait()


def fused(layer_input, output_grad, key_weight, adapter_down, adapter_up, segment_adapter, adapter_slot, live_segments):
    T, Q = lax.axis_size("tensor"), lax.axis_size("dp")
    X = 1 << ((T.bit_length() - 1) // 2)
    W = layer_input.shape[1]
    L, K = output_grad.shape
    PO, R, KS = adapter_up.shape
    S = segment_adapter.shape[0] // Q
    Y = Q // 2
    dims = (T, X, Q, S, L, R, W, K, KS, PO)
    bf, f32 = jnp.bfloat16, jnp.float32
    V, DMA = pltpu.VMEM, pltpu.SemaphoreType.DMA
    far_in = pl.BlockSpec(memory_space=pltpu.HBM)
    hbm = pl.BlockSpec(memory_space=pl.ANY)
    flops = 2 * T * L * K * W + 8 * T * L * R * W
    input_grad, down_grad, up_grad = pl.pallas_call(
        functools.partial(fused_kernel, dims),
        out_shape=(
            jax.ShapeDtypeStruct((T, L, W), bf),
            jax.ShapeDtypeStruct((PO, R, W), bf),
            jax.ShapeDtypeStruct((PO, R, KS), bf),
        ),
        in_specs=[far_in] * 8,
        out_specs=(hbm,) * 3,
        scratch_shapes=[
            pltpu.SMEM((Q * S,), jnp.int32), pltpu.SMEM((adapter_slot.shape[0],), jnp.int32),
            pltpu.SMEM((1,), jnp.int32), pltpu.SMEM((Q * S,), jnp.int32),
            pltpu.SMEM((PO * Q,), jnp.int32),
            V((T, L, W), bf), V((W, K), bf), V((PO, R, W), bf), V((PO, R, KS), bf), V((L, K), bf),
            V((T, L, K), bf), V((T, L, W), bf), V((PO, R, W), bf), V((PO, R, KS), bf),
            V((Y, S, R, W), bf), V((Y, S, R, W), bf), V((Y, S, R, W), bf), V((Y, S, R, W), bf),
            V((Q, S, R, KS), bf), V((Q, S, R, KS), bf),
            V((S, R, W), bf), V((S, R, KS), bf), V((T, R, KS), bf), V((T, R, L), bf),
            V((S, R, L), f32), V((T, R, L), f32), V((T, R, KS), f32), V((T, R, KS), f32),
            V((Q, S, R, W), bf), V((Q, S, R, KS), bf),
            DMA((8,)), DMA((T + 2,)), DMA((T, CHUNKS, 1 + X)), DMA((T, CHUNKS)),
            DMA((2,)), DMA((2,)), DMA((Y, 2)), DMA((Y, 2)), DMA((Q,)), DMA((Q,)),
            DMA((T,)), DMA((T,)), DMA((T,)), DMA((T,)),
            DMA((T,)), DMA((T,)), DMA((T,)), DMA((T,)),
            DMA((Y,)), DMA((Q,)), DMA((Q,)), DMA((Q, 2)),
        ],
        compiler_params=pltpu.CompilerParams(
            collective_id=0, has_side_effects=True, vmem_limit_bytes=VMEM_LIMIT
        ),
        cost_estimate=pl.CostEstimate(
            flops=flops, bytes_accessed=2 * (2 * T * L * W + K * W + 2 * PO * R * W), transcendentals=0
        ),
    )(
        segment_adapter, adapter_slot, live_segments,
        layer_input.reshape(T, L, W), output_grad, key_weight, adapter_down, adapter_up,
    )
    results = (input_grad, down_grad, up_grad)
    input_grad, down_grad, up_grad = pl.pallas_call(
        store_kernel,
        out_shape=tuple(jax.ShapeDtypeStruct(r.shape, r.dtype) for r in results),
        in_specs=[hbm] * 3,
        out_specs=(hbm,) * 3,
        scratch_shapes=[DMA((7,))],
        compiler_params=pltpu.CompilerParams(vmem_limit_bytes=VMEM_LIMIT),
        cost_estimate=pl.CostEstimate(
            flops=0, bytes_accessed=4 * (T * L * W + PO * R * W), transcendentals=0
        ),
    )(*results)
    return input_grad.reshape(T * L, W), down_grad, up_grad


def on_device(
    layer_input,
    output_grad,
    key_weight,
    adapter_down,
    adapter_up,
    segment_adapter,
    adapter_slot,
    live_segments,
):
    tensor_size = lax.axis_size("tensor")
    position = lax.axis_index("tensor")
    group_count = lax.axis_size("dp")
    group_index = lax.axis_index("dp")
    row_count = output_grad.shape[0]
    tok_group = layer_input.shape[0]
    width_shard = layer_input.shape[1]
    key_width = output_grad.shape[1]
    key_shard = key_width // tensor_size
    adapters = adapter_slot.shape[0]
    rank_dim = adapter_down.shape[1]
    seg_total = segment_adapter.shape[0]
    seg_group = seg_total // group_count
    seg_len = tok_group // seg_group
    per_owner = adapters // group_count
    slot_ids = jnp.arange(adapters, dtype=jnp.int32)
    lookup = segment_adapter[:, None] == slot_ids[None, :]
    every_slot = jnp.sum(jnp.where(lookup, adapter_slot[None, :], 0), axis=1)
    seg_slot = lax.dynamic_slice_in_dim(every_slot, group_index * seg_group, seg_group)
    local_rows = position * row_count + jnp.arange(row_count, dtype=jnp.int32)
    live_rows = local_rows // seg_len < live_segments[0]
    masked = jnp.where(live_rows[:, None], output_grad, jnp.zeros_like(output_grad))
    whole = lax.all_gather(masked, "tensor", axis=0, tiled=True)
    stores = (
        lax.all_gather(adapter_down, "dp", axis=0, tiled=True),
        lax.all_gather(adapter_up, "dp", axis=0, tiled=True),
    )
    choose = (seg_slot[:, None] == slot_ids[None, :]).astype(jnp.bfloat16)
    down_seg = jnp.dot(choose, stores[0].reshape(adapters, -1), preferred_element_type=jnp.float32)
    down_seg = down_seg.astype(jnp.bfloat16).reshape(seg_group, rank_dim, width_shard)
    up_seg = jnp.dot(choose, stores[1].reshape(adapters, -1), preferred_element_type=jnp.float32)
    up_seg = up_seg.astype(jnp.bfloat16).reshape(seg_group, rank_dim, key_shard)
    own_keys = lax.dynamic_slice_in_dim(whole, position * key_shard, key_shard, 1).reshape(
        seg_group, seg_len, key_shard
    )
    input_seg = layer_input.reshape(seg_group, seg_len, width_shard)
    up_part = jnp.einsum("sjk,srk->rsj", own_keys, up_seg, preferred_element_type=jnp.float32)
    down_part = jnp.einsum("sjd,srd->rsj", input_seg, down_seg, preferred_element_type=jnp.float32)
    lowrank, projected = lax.psum((up_part, down_part), "tensor")
    lowrank = lowrank.astype(jnp.bfloat16)
    projected = projected.astype(jnp.bfloat16)
    frozen = lax.dot_general(
        whole, key_weight, (((1,), (1,)), ((), ())), preferred_element_type=jnp.float32
    )
    extra = jnp.einsum("rsj,srd->sjd", lowrank, down_seg, preferred_element_type=jnp.float32)
    input_grad = (frozen + 2.0 * extra.reshape(tok_group, width_shard)).astype(jnp.bfloat16)
    seg_down = 2.0 * jnp.einsum(
        "rsj,sjd->srd", lowrank, input_seg, preferred_element_type=jnp.float32
    )
    seg_up = 2.0 * jnp.einsum(
        "rsj,sjk->srk", projected, own_keys, preferred_element_type=jnp.float32
    )
    seg_index = jnp.arange(seg_group, dtype=jnp.int32)
    same = seg_slot[:, None] == seg_slot[None, :]
    earlier = same & (seg_index[None, :] < seg_index[:, None])
    leading = jnp.logical_not(jnp.any(earlier, axis=1))
    merge_rows = (same & leading[:, None]).astype(jnp.float32)
    rows_down = jnp.einsum(
        "us,srd->urd", merge_rows, seg_down, precision=lax.Precision.HIGHEST
    ).astype(jnp.bfloat16)
    rows_up = jnp.einsum("us,srk->urk", merge_rows, seg_up, precision=lax.Precision.HIGHEST).astype(
        jnp.bfloat16
    )
    every_down, every_up = (
        lax.all_gather(rows_down, "dp", axis=0, tiled=True),
        lax.all_gather(rows_up, "dp", axis=0, tiled=True),
    )
    owned = group_index * per_owner + jnp.arange(per_owner, dtype=jnp.int32)
    mine = (every_slot[:, None] == owned[None, :]).astype(jnp.bfloat16)
    down_grad = jnp.einsum(
        "sp,srd->prd", mine, every_down, preferred_element_type=jnp.float32
    ).astype(jnp.bfloat16)
    up_grad = jnp.einsum("sp,srk->prk", mine, every_up, preferred_element_type=jnp.float32).astype(
        jnp.bfloat16
    )
    return (input_grad, down_grad, up_grad)


def device_program(layer_input, output_grad, key_weight, adapter_down, adapter_up, segment_adapter, adapter_slot, live_segments):
    args = (layer_input, output_grad, key_weight, adapter_down, adapter_up, segment_adapter, adapter_slot, live_segments)
    seg_group = segment_adapter.shape[0] // lax.axis_size("dp")
    one_each = seg_group == lax.axis_size("tensor")
    tiled = adapter_up.shape[2] % 128 == 0 and layer_input.shape[1] % 256 == 0
    if one_each and tiled and lax.axis_size("dp") % 2 == 0:
        return fused(*args)
    return on_device(*args)


def solution(mesh):
    in_specs = (
        P("dp", "tensor"),
        P(("dp", "tensor"), None),
        P("tensor", None),
        P("dp", None, "tensor"),
        P("dp", None, "tensor"),
        P(),
        P(),
        P("dp"),
    )
    out_specs = (P("dp", "tensor"), P("dp", None, "tensor"), P("dp", None, "tensor"))
    return jax.shard_map(
        device_program, mesh=mesh, in_specs=in_specs, out_specs=out_specs, check_vma=False
    )
```

profile of v0, /device:TPU:0, one launch (start us, length us, event | category | flops | bytes accessed | tf_op | source)
XLA Modules:
  0.0 142.0 jit_solution(14049776394717961562)
XLA Ops:
  1.3 40.3 %shard_map.103 = (bf16[8,128,1024]{2,1,0:T(8,128)(2,1)}, bf16[32,16,1024]{2,1,0:T(8,128)(2,1)}, bf16[32,16,128]{2,1,0:T(8,128)(2,1)}) custom-call(s32[32]{0:T(128)} %adapter_hbm.1, s32[128]{0:T(128)} %slot_hbm.1, s32[1]{0:T(128)S(6)} %copy.11.live_hbm, bf16[8,128,1024]{2,1,0:T(8,128)(2,1)} %bitcast.2, bf16[128,1024]{1,0:T(8,128)(2,1)} %og_hbm.1, ...), custom_call_target="tpu_custom_call" | custom-call | flops 2281701376 | bytes 8388608 | tf_op jit(solution)/shard_map/pallas_call | solution.py:422
  41.5 100.4 %shard_map.104 = (bf16[8,128,1024]{2,1,0:T(8,128)(2,1)}, bf16[32,16,1024]{2,1,0:T(8,128)(2,1)}, bf16[32,16,128]{2,1,0:T(8,128)(2,1)}) custom-call(bf16[8,128,1024]{2,1,0:T(8,128)(2,1)} %get-tuple-element.9.a, bf16[32,16,1024]{2,1,0:T(8,128)(2,1)} %get-tuple-element.10.b, bf16[32,16,128]{2,1,0:T(8,128)(2,1)} %get-tuple-element.11.c), custom_call_target="tpu_custom_call" | custom-call | bytes 6291456 | tf_op jit(solution)/shard_map/pallas_call | solution.py:459
where the time goes:
time: 142 us
  Pallas kernels  141 us (99%)
    pallas_call x1, Pallas kernels, fused(): pl.pallas_call(store_kernel, out_shape=tuple((jax.ShapeDtypeStruct(r.shap...  100 us
    pallas_call x1, Pallas kernels, fused(): pl.pallas_call(functools.partial(fused_kernel, dims), out_shape=(jax.Shap...  40.3 us

commit v1 on v0

--- a/solution.py
+++ b/solution.py
@@ -80,13 +80,48 @@
     for peer in dp_peers:
         pl.semaphore_signal(barrier, inc=1, device_id={"dp": peer}, device_id_type=MESH)
 
+    for copy in scalars[:2]:
+        copy.wait()
+    for s in range(Q * S):
+        seg_slot[s] = slot_s[adapter_s[s]]
+
+    def owned(index):
+        local = seg_slot[index] - q * PO
+        inside = jnp.logical_and(local >= 0, local < PO)
+        return inside, jnp.clip(local, 0, PO - 1)
+
+    loads[2].wait()
+
+    def choose_down(i, carry):
+        group, s = i // S, lax.rem(i, S)
+        inside, local = owned((group * 2 + 1 - c) * S + s)
+        s1d_out[group, s] = jnp.where(inside, ad_v[local], jnp.zeros((R, W), jnp.bfloat16))
+        return carry
+
+    lax.fori_loop(0, Y * S, choose_down, 0)
+    loads[1].wait()
+
+    def choose_up(i, carry):
+        group, s = i // S, lax.rem(i, S)
+        inside, local = owned(i)
+        fu_out[group, s] = jnp.where(inside, au_v[local], jnp.zeros((R, KS), jnp.bfloat16))
+        return carry
+
+    lax.fori_loop(0, Q * S, choose_up, 0)
+    pl.semaphore_wait(barrier, T - 1 + Q - 1)
+
+    for copy in later_loads:
+        copy.start()
+    send(s1d_out, s1d_in, s1_send.at[0], s1_recv.at[0], {"dp": mate})
+
+    for peer in dp_peers:
+        send(fu_out.at[peer], fu_in.at[q], fu_send.at[peer], fu_recv.at[q], {"dp": peer})
+
     scalars[2].wait()
     loads[0].wait()
     live = t < live_s[0]
     own_rows = jnp.where(live, og_v[...], jnp.zeros((L, K), jnp.bfloat16))
     whole[t] = own_rows
-
-    pl.semaphore_wait(barrier, T - 1 + Q - 1)
 
     def rows_of(origin, part):
         return whole.at[origin, pl.ds(part * half, half)]
@@ -110,10 +145,12 @@
     direct = CHUNKS // 2 if paired else CHUNKS
     pair_z = z + 1 - 2 * lax.rem(z, 2)
     column = z * X + lax.rem(x + 1, X)
-    for part in range(CHUNKS):
+    def start_own(part):
         to_z(t, part, True, None)
         to_z(t, part, False, None)
         to_x(t, part, None)
+
+    start_own(0)
 
     def forward(step, part):
         for sign in (-1, 1):
@@ -134,40 +171,11 @@
             send(ref, ref, blk_send.at[column, part, 0], blk_recv.at[column, part],
                  {"tensor": pair_z * X + x})
 
-    for copy in scalars[:2]:
-        copy.wait()
-    for s in range(Q * S):
-        seg_slot[s] = slot_s[adapter_s[s]]
-
-    def owned(index):
-        local = seg_slot[index] - q * PO
-        inside = jnp.logical_and(local >= 0, local < PO)
-        return inside, jnp.clip(local, 0, PO - 1)
-
-    loads[1].wait()
-
-    def choose_up(i, carry):
+    def combine_down(i, carry):
         group, s = i // S, lax.rem(i, S)
-        inside, local = owned(i)
-        fu_out[group, s] = jnp.where(inside, au_v[local], jnp.zeros((R, KS), jnp.bfloat16))
+        inside, local = owned((group * 2 + c) * S + s)
+        s2d_out[group, s] = jnp.where(inside, ad_v[local], s1d_in[group, s])
         return carry
-
-    lax.fori_loop(0, Q * S, choose_up, 0)
-    for peer in dp_peers:
-        send(fu_out.at[peer], fu_in.at[q], fu_send.at[peer], fu_recv.at[q], {"dp": peer})
-
-    loads[2].wait()
-
-    def choose_down(i, carry):
-        group, s = i // S, lax.rem(i, S)
-        inside, local = owned((group * 2 + 1 - c) * S + s)
-        s1d_out[group, s] = jnp.where(inside, ad_v[local], jnp.zeros((R, W), jnp.bfloat16))
-        return carry
-
-    lax.fori_loop(0, Y * S, choose_down, 0)
-    for copy in later_loads:
-        copy.start()
-    send(s1d_out, s1d_in, s1_send.at[0], s1_recv.at[0], {"dp": mate})
 
     def first_of(p, carry):
         slot = q * PO + p
@@ -180,19 +188,21 @@
 
     lax.fori_loop(0, PO, first_of, 0)
 
-    def combine_down(i, carry):
-        group, s = i // S, lax.rem(i, S)
-        inside, local = owned((group * 2 + c) * S + s)
-        s2d_out[group, s] = jnp.where(inside, ad_v[local], s1d_in[group, s])
-        return carry
-
     arrived(s1d_in, s1_recv.at[0])
-    lax.fori_loop(0, Y * S, combine_down, 0)
-    for other in far:
-        send(s2d_out.at[other], s2d_in.at[y], s2_send.at[other, 0], s2_recv.at[y, 0],
-             {"dp": other * 2 + c})
-
-    forward(1, 0)
+    part_segs = S // 2
+
+    def segs(piece):
+        return pl.ds(piece * part_segs, part_segs)
+
+    for piece in range(2):
+        def combine_piece(i, carry):
+            return combine_down(i // part_segs * S + piece * part_segs + lax.rem(i, part_segs), carry)
+
+        lax.fori_loop(0, Y * part_segs, combine_piece, 0)
+        for other in far:
+            send(s2d_out.at[other, segs(piece)], s2d_in.at[y, segs(piece)], s2_send.at[other, piece],
+                 s2_recv.at[y, piece], {"dp": other * 2 + c})
+    start_own(1)
 
     total = fu_out[q]
     for peer in dp_peers:
@@ -203,8 +213,8 @@
         send(up_seg.at[peer], up_own.at[t], up_send.at[peer], up_recv.at[t], {"tensor": peer})
     up_own[t] = up_seg[t]
 
-    forward(1, 1)
-    forward(1, 2)
+    start_own(2)
+    forward(1, 0)
 
     for peer in tensor_peers:
         arrived(up_own.at[peer], up_recv.at[peer])
@@ -217,14 +227,11 @@
     for peer in tensor_peers:
         send(lr.at[t], lr.at[t], lr_send.at[peer], lr_recv.at[t], {"tensor": peer})
 
+    start_own(3)
+    forward(1, 1)
     share(2)
-    forward(1, 3)
-    share(3)
-    if Z > 2:
-        forward(2, 0)
-
-    for other in far:
-        arrived(s2d_in.at[other], s2_recv.at[other, 0])
+    forward(1, 2)
+
     later_loads[0].wait()
 
     def down_of(s, carry):
@@ -235,13 +242,21 @@
         pr_out[s] = lax.dot_general(rows, x_v[s], NT, preferred_element_type=jnp.float32)
         return carry
 
-    lax.fori_loop(0, S, down_of, 0)
-    for peer in tensor_peers:
-        send(pr_out.at[peer], pr_in.at[t], pr_send.at[peer], pr_recv.at[t], {"tensor": peer})
-    pr_in[t] = pr_out[t]
-
-    if Z > 2:
-        forward(2, 1)
+    def project(piece):
+        for other in far:
+            arrived(s2d_in.at[other, segs(piece)], s2_recv.at[other, piece])
+        lax.fori_loop(piece * part_segs, (piece + 1) * part_segs, down_of, 0, unroll=2)
+        for s in range(piece * part_segs, (piece + 1) * part_segs):
+            remote = s != t
+            send(pr_out.at[s], pr_in.at[t], pr_send.at[s], pr_recv.at[t], {"tensor": s}, remote)
+
+            @pl.when(s == t)
+            def _():
+                pr_in[t] = pr_out[s]
+
+    project(0)
+    forward(1, 3)
+    share(3)
 
     for peer in tensor_peers:
         arrived(lr.at[peer], lr_recv.at[peer])
@@ -267,6 +282,11 @@
              {"dp": other * 2 + c})
     send(rows_d.at[q], rows_d.at[q], rwc_send.at[q], rw_recv.at[q, 0], {"dp": mate})
 
+    if Z > 2:
+        forward(2, 0)
+    project(1)
+    if Z > 2:
+        forward(2, 1)
     if Z > 2:
         forward(2, 2)
 
@@ -352,33 +372,38 @@
     for group in range(Y):
         origin = group * 2 + 1 - c
         arrived(rows_d.at[origin], rw_recv.at[origin, 0])
-    for peer in dp_peers:
-        arrived(rows_u.at[peer], rw_recv.at[peer, 1])
-
-    def owner_rows(p, carry):
-        down_total = jnp.zeros((R, W), jnp.float32)
-        up_total = jnp.zeros((R, KS), jnp.float32)
+
+    def owner_sum(rows, out, p, width):
+        total = jnp.zeros((R, width), jnp.float32)
         for group in range(Q):
             index = first[p * Q + group]
-            has = index >= 0
-            index = jnp.maximum(index, 0)
-            down_total += jnp.where(has, rows_d[group, index].astype(jnp.float32), 0.0)
-            up_total += jnp.where(has, rows_u[group, index].astype(jnp.float32), 0.0)
-        dg_v[p] = down_total.astype(jnp.bfloat16)
-        ug_v[p] = up_total.astype(jnp.bfloat16)
+            row = rows[group, jnp.maximum(index, 0)].astype(jnp.float32)
+            total += jnp.where(index >= 0, row, 0.0)
+        out[p] = total.astype(jnp.bfloat16)
+
+    def owner_down(p, carry):
+        owner_sum(rows_d, dg_v, p, W)
         return carry
 
-    lax.fori_loop(0, PO, owner_rows, 0, unroll=2)
+    def owner_up(p, carry):
+        owner_sum(rows_u, ug_v, p, KS)
+        return carry
+
+    lax.fori_loop(0, PO, owner_down, 0, unroll=2)
     stores = [
         pltpu.make_async_copy(dg_v, dg_hbm, store_sem.at[Z]),
         pltpu.make_async_copy(ug_v, ug_hbm, store_sem.at[Z + 1]),
     ]
-    for copy in stores:
-        copy.start()
+    stores[0].start()
 
     if Z > 2:
         wait_side(nearest(Z - 1), range(CHUNKS))
         block_row(nearest(Z - 1))
+
+    for peer in dp_peers:
+        arrived(rows_u.at[peer], rw_recv.at[peer, 1])
+    lax.fori_loop(0, PO, owner_up, 0, unroll=4)
+    stores[1].start()
 
     for when, copy in pending:
         if when is None:
@@ -392,17 +417,23 @@
         copy.wait()
 
 
-def store_kernel(a, b, c, a_out, b_out, c_out, sem):
-    copies = [pltpu.make_async_copy(c, c_out, sem.at[0])]
-    for src, dst, pieces in ((a, a_out, 4), (b, b_out, 2)):
+def store_kernel(a, b, c, a_out, b_out, c_out, a_v, b_v, c_v, in_sem, out_sem):
+    moves = []
+    for src, held, dst, pieces in ((a, a_v, a_out, 4), (b, b_v, b_out, 2), (c, c_v, c_out, 1)):
         count = src.shape[0] // pieces
         for i in range(pieces):
-            at = pl.ds(i * count, count)
-            copies.append(pltpu.make_async_copy(src.at[at], dst.at[at], sem.at[len(copies)]))
-    for copy in copies:
-        copy.start()
-    for copy in copies:
-        copy.wait()
+            at, n = pl.ds(i * count, count), len(moves)
+            moves.append((
+                pltpu.make_async_copy(src.at[at], held.at[at], in_sem.at[n]),
+                pltpu.make_async_copy(held.at[at], dst.at[at], out_sem.at[n]),
+            ))
+    for load, _ in moves:
+        load.start()
+    for load, store in moves:
+        load.wait()
+        store.start()
+    for _, store in moves:
+        store.wait()
 
 
 def fused(layer_input, output_grad, key_weight, adapter_down, adapter_up, segment_adapter, adapter_slot, live_segments):
@@ -461,7 +492,7 @@
         out_shape=tuple(jax.ShapeDtypeStruct(r.shape, r.dtype) for r in results),
         in_specs=[hbm] * 3,
         out_specs=(hbm,) * 3,
-        scratch_shapes=[DMA((7,))],
+        scratch_shapes=[V(r.shape, r.dtype) for r in results] + [DMA((7,)), DMA((7,))],
         compiler_params=pltpu.CompilerParams(vmem_limit_bytes=VMEM_LIMIT),
         cost_estimate=pl.CostEstimate(
             flops=0, bytes_accessed=4 * (T * L * W + PO * R * W), transcendentals=0

time: 142 us -> 45.9 us (0.32)
  Pallas kernels: 141 us -> 44.5 us
    pallas_call x1, Pallas kernels: 100 us -> 2.85 us  [fused(): pl.pallas_call(store_kernel, out_shape=tuple((jax.ShapeDtypeStruct(r.shap...]
where the time goes in v1:
time: 45.9 us; the launch traced here: 45.7 us
  Pallas kernels  44.5 us (97%)
  between operations  1.29 us (3%)
    pallas_call x1, Pallas kernels, fused(): pl.pallas_call(functools.partial(fused_kernel, dims), out_shape=(jax.Shap...  41.6 us
    pallas_call x1, Pallas kernels, fused(): pl.pallas_call(store_kernel, out_shape=tuple((jax.ShapeDtypeStruct(r.shap...  2.85 us

profile of v1, /device:TPU:0, one launch (start us, length us, event | category | flops | bytes accessed | tf_op | source)
XLA Modules:
  0.0 45.7 jit_solution(397087448924065604)
XLA Ops:
  1.3 41.6 %shard_map.103 = (bf16[8,128,1024]{2,1,0:T(8,128)(2,1)}, bf16[32,16,1024]{2,1,0:T(8,128)(2,1)}, bf16[32,16,128]{2,1,0:T(8,128)(2,1)}) custom-call(s32[32]{0:T(128)} %adapter_hbm.1, s32[128]{0:T(128)} %slot_hbm.1, s32[1]{0:T(128)S(6)} %copy.11.live_hbm, bf16[8,128,1024]{2,1,0:T(8,128)(2,1)} %bitcast.2, bf16[128,1024]{1,0:T(8,128)(2,1)} %og_hbm.1, ...), custom_call_target="tpu_custom_call" | custom-call | flops 2281701376 | bytes 8388608 | tf_op jit(solution)/shard_map/pallas_call | solution.py:453
  42.9 2.9 %shard_map.104 = (bf16[8,128,1024]{2,1,0:T(8,128)(2,1)}, bf16[32,16,1024]{2,1,0:T(8,128)(2,1)}, bf16[32,16,128]{2,1,0:T(8,128)(2,1)}) custom-call(bf16[8,128,1024]{2,1,0:T(8,128)(2,1)} %get-tuple-element.9.a, bf16[32,16,1024]{2,1,0:T(8,128)(2,1)} %get-tuple-element.10.b, bf16[32,16,128]{2,1,0:T(8,128)(2,1)} %get-tuple-element.11.c), custom_call_target="tpu_custom_call" | custom-call | bytes 6291456 | tf_op jit(solution)/shard_map/pallas_call | solution.py:490

commit v2 on v1

--- a/solution.py
+++ b/solution.py
@@ -80,48 +80,12 @@
     for peer in dp_peers:
         pl.semaphore_signal(barrier, inc=1, device_id={"dp": peer}, device_id_type=MESH)
 
-    for copy in scalars[:2]:
-        copy.wait()
-    for s in range(Q * S):
-        seg_slot[s] = slot_s[adapter_s[s]]
-
-    def owned(index):
-        local = seg_slot[index] - q * PO
-        inside = jnp.logical_and(local >= 0, local < PO)
-        return inside, jnp.clip(local, 0, PO - 1)
-
-    loads[2].wait()
-
-    def choose_down(i, carry):
-        group, s = i // S, lax.rem(i, S)
-        inside, local = owned((group * 2 + 1 - c) * S + s)
-        s1d_out[group, s] = jnp.where(inside, ad_v[local], jnp.zeros((R, W), jnp.bfloat16))
-        return carry
-
-    lax.fori_loop(0, Y * S, choose_down, 0)
-    loads[1].wait()
-
-    def choose_up(i, carry):
-        group, s = i // S, lax.rem(i, S)
-        inside, local = owned(i)
-        fu_out[group, s] = jnp.where(inside, au_v[local], jnp.zeros((R, KS), jnp.bfloat16))
-        return carry
-
-    lax.fori_loop(0, Q * S, choose_up, 0)
-    pl.semaphore_wait(barrier, T - 1 + Q - 1)
-
-    for copy in later_loads:
-        copy.start()
-    send(s1d_out, s1d_in, s1_send.at[0], s1_recv.at[0], {"dp": mate})
-
-    for peer in dp_peers:
-        send(fu_out.at[peer], fu_in.at[q], fu_send.at[peer], fu_recv.at[q], {"dp": peer})
-
     scalars[2].wait()
     loads[0].wait()
     live = t < live_s[0]
     own_rows = jnp.where(live, og_v[...], jnp.zeros((L, K), jnp.bfloat16))
     whole[t] = own_rows
+    pl.semaphore_wait(barrier, T - 1 + Q - 1)
 
     def rows_of(origin, part):
         return whole.at[origin, pl.ds(part * half, half)]
@@ -141,8 +105,7 @@
             send(ref, ref, blk_send.at[origin, part, 1 + j], blk_recv.at[origin, part],
                  {"tensor": to}, when)
 
-    paired = X == 2 and Z % 2 == 0
-    direct = CHUNKS // 2 if paired else CHUNKS
+    direct = CHUNKS // 2
     pair_z = z + 1 - 2 * lax.rem(z, 2)
     column = z * X + lax.rem(x + 1, X)
     def start_own(part):
@@ -151,6 +114,7 @@
         to_x(t, part, None)
 
     start_own(0)
+    start_own(1)
 
     def forward(step, part):
         for sign in (-1, 1):
@@ -165,17 +129,52 @@
             to_x(origin, part, across)
 
     def share(part):
-        if paired:
-            ref = rows_of(column, part)
-            arrived(ref, blk_recv.at[column, part])
-            send(ref, ref, blk_send.at[column, part, 0], blk_recv.at[column, part],
-                 {"tensor": pair_z * X + x})
+        ref = rows_of(column, part)
+        send(ref, ref, blk_send.at[column, part, 0], blk_recv.at[column, part],
+             {"tensor": pair_z * X + x})
 
     def combine_down(i, carry):
         group, s = i // S, lax.rem(i, S)
         inside, local = owned((group * 2 + c) * S + s)
         s2d_out[group, s] = jnp.where(inside, ad_v[local], s1d_in[group, s])
         return carry
+
+    for copy in scalars[:2]:
+        copy.wait()
+    for s in range(Q * S):
+        seg_slot[s] = slot_s[adapter_s[s]]
+
+    def owned(index):
+        local = seg_slot[index] - q * PO
+        inside = jnp.logical_and(local >= 0, local < PO)
+        return inside, jnp.clip(local, 0, PO - 1)
+
+    loads[2].wait()
+
+    def choose_down(i, carry):
+        group, s = i // S, lax.rem(i, S)
+        inside, local = owned((group * 2 + 1 - c) * S + s)
+        s1d_out[group, s] = jnp.where(inside, ad_v[local], jnp.zeros((R, W), jnp.bfloat16))
+        return carry
+
+    lax.fori_loop(0, Y * S, choose_down, 0)
+    loads[1].wait()
+
+    def choose_up(i, carry):
+        group, s = i // S, lax.rem(i, S)
+        inside, local = owned(i)
+        fu_out[group, s] = jnp.where(inside, au_v[local], jnp.zeros((R, KS), jnp.bfloat16))
+        return carry
+
+    lax.fori_loop(0, Q * S, choose_up, 0)
+    for copy in later_loads:
+        copy.start()
+    send(s1d_out, s1d_in, s1_send.at[0], s1_recv.at[0], {"dp": mate})
+
+    for peer in dp_peers:
+        send(fu_out.at[peer], fu_in.at[q], fu_send.at[peer], fu_recv.at[q], {"dp": peer})
+    start_own(2)
+    start_own(3)
 
     def first_of(p, carry):
         slot = q * PO + p
@@ -202,8 +201,6 @@
         for other in far:
             send(s2d_out.at[other, segs(piece)], s2d_in.at[y, segs(piece)], s2_send.at[other, piece],
                  s2_recv.at[y, piece], {"dp": other * 2 + c})
-    start_own(1)
-
     total = fu_out[q]
     for peer in dp_peers:
         arrived(fu_in.at[peer], fu_recv.at[peer])
@@ -213,7 +210,6 @@
         send(up_seg.at[peer], up_own.at[t], up_send.at[peer], up_recv.at[t], {"tensor": peer})
     up_own[t] = up_seg[t]
 
-    start_own(2)
     forward(1, 0)
 
     for peer in tensor_peers:
@@ -227,9 +223,7 @@
     for peer in tensor_peers:
         send(lr.at[t], lr.at[t], lr_send.at[peer], lr_recv.at[t], {"tensor": peer})
 
-    start_own(3)
     forward(1, 1)
-    share(2)
     forward(1, 2)
 
     later_loads[0].wait()
@@ -256,7 +250,6 @@
 
     project(0)
     forward(1, 3)
-    share(3)
 
     for peer in tensor_peers:
         arrived(lr.at[peer], lr_recv.at[peer])
@@ -282,47 +275,35 @@
              {"dp": other * 2 + c})
     send(rows_d.at[q], rows_d.at[q], rwc_send.at[q], rw_recv.at[q, 0], {"dp": mate})
 
-    if Z > 2:
-        forward(2, 0)
+    forward(2, 0)
     project(1)
-    if Z > 2:
-        forward(2, 1)
-    if Z > 2:
-        forward(2, 2)
-
+    forward(2, 1)
     later_loads[1].wait()
 
-    def block_row(row):
-        left_rows = whole[pl.ds(row * X, X)].reshape(X * L, K)
+    def two_blocks(pair):
+        left_rows = jnp.concatenate([whole[origin] for origin in pair], axis=0)
         for n in range(W // tile):
             at = slice(n * tile, (n + 1) * tile)
             value = lax.dot_general(left_rows, kw_v[at, :], NT, preferred_element_type=jnp.float32)
-            for j in range(X):
-                origin = row * X + j
+            for j, origin in enumerate(pair):
                 extra = lax.dot_general(
                     lr[origin], down_seg[origin, :, at], TN, preferred_element_type=jnp.float32
                 )
                 ig_v[origin, :, at] = (value[j * L:(j + 1) * L] + 2.0 * extra).astype(jnp.bfloat16)
-        rows = pl.ds(row * X, X)
-        pltpu.make_async_copy(ig_v.at[rows], ig_hbm.at[rows], store_sem.at[row]).start()
-
-    def wait_side(row, parts):
-        for j in range(1, X):
-            origin = row * X + lax.rem(x + j, X)
-            for part in parts:
-                arrived(rows_of(origin, part), blk_recv.at[origin, part])
-
-    def nearest(i):
-        low, high = z, Z - 1 - z
-        both = jnp.minimum(low, high)
-        near = z + (-1 if i % 2 else 1) * ((i + 1) // 2)
-        beyond = jnp.where(low < high, z + (i - both), z - (i - both))
-        return jnp.where(i <= 2 * both, near, beyond)
-
-    wait_side(z, range(direct))
-    block_row(z)
-    if Z > 2:
-        forward(2, 3)
+        for origin in pair:
+            pltpu.make_async_copy(ig_v.at[origin], ig_hbm.at[origin], store_sem.at[origin]).start()
+
+    def wait_side(origin, parts):
+        for part in parts:
+            arrived(rows_of(origin, part), blk_recv.at[origin, part])
+
+    lower = z < 2
+    near_row, far_row = jnp.where(lower, 2, 1), jnp.where(lower, 3, 0)
+    other = lax.rem(x + 1, X)
+
+    wait_side(column, range(CHUNKS))
+    two_blocks((t, column))
+    forward(2, 2)
 
     for peer in tensor_peers:
         arrived(pr_in.at[peer], pr_recv.at[peer])
@@ -338,12 +319,12 @@
         send(su_out.at[peer], su_in.at[t], su_send.at[peer], su_recv.at[t], {"tensor": peer})
     su_in[t] = su_out[t]
 
-    for step in range(3, Z):
-        forward(step, 0)
-    wait_side(nearest(1), range(CHUNKS))
-    block_row(nearest(1))
-    for step in range(3, Z):
-        forward(step, 1)
+    forward(2, 3)
+    for part in range(direct, CHUNKS):
+        share(part)
+    forward(3, 0)
+    two_blocks((pair_z * X + x, near_row * X + x))
+    forward(3, 1)
 
     for peer in tensor_peers:
         arrived(su_in.at[peer], su_recv.at[peer])
@@ -356,18 +337,15 @@
     for peer in dp_peers:
         send(rows_u.at[q], rows_u.at[q], rwu_send.at[peer], rw_recv.at[q, 1], {"dp": peer})
 
-    for i in range(2, Z - 1):
-        wait_side(nearest(i), range(CHUNKS))
-        block_row(nearest(i))
-    for step in range(3, Z):
-        forward(step, 2)
-    for other in far:
-        origin = other * 2 + c
+    forward(3, 2)
+    for far_chip in far:
+        origin = far_chip * 2 + c
         arrived(rows_d.at[origin], rw_recv.at[origin, 0])
         send(rows_d.at[origin], rows_d.at[origin], rwc_send.at[origin],
              rw_recv.at[origin, 0], {"dp": mate})
-    for step in range(3, Z):
-        forward(step, 3)
+    forward(3, 3)
+    wait_side(near_row * X + other, range(CHUNKS))
+    two_blocks((far_row * X + x, near_row * X + other))
 
     for group in range(Y):
         origin = group * 2 + 1 - c
@@ -391,14 +369,14 @@
 
     lax.fori_loop(0, PO, owner_down, 0, unroll=2)
     stores = [
-        pltpu.make_async_copy(dg_v, dg_hbm, store_sem.at[Z]),
-        pltpu.make_async_copy(ug_v, ug_hbm, store_sem.at[Z + 1]),
+        pltpu.make_async_copy(dg_v, dg_hbm, store_sem.at[T]),
+        pltpu.make_async_copy(ug_v, ug_hbm, store_sem.at[T + 1]),
     ]
     stores[0].start()
 
-    if Z > 2:
-        wait_side(nearest(Z - 1), range(CHUNKS))
-        block_row(nearest(Z - 1))
+    wait_side(far_row * X + other, range(CHUNKS))
+    wait_side(pair_z * X + other, range(CHUNKS))
+    two_blocks((pair_z * X + other, far_row * X + other))
 
     for peer in dp_peers:
         arrived(rows_u.at[peer], rw_recv.at[peer, 1])
@@ -410,9 +388,8 @@
             copy.wait_send()
         else:
             pl.when(when)(copy.wait_send)
-    for row in range(Z):
-        rows = pl.ds(row * X, X)
-        pltpu.make_async_copy(ig_v.at[rows], ig_hbm.at[rows], store_sem.at[row]).wait()
+    for origin in range(T):
+        pltpu.make_async_copy(ig_v.at[origin], ig_hbm.at[origin], store_sem.at[origin]).wait()
     for copy in stores:
         copy.wait()
 
@@ -592,7 +569,7 @@
 def device_program(layer_input, output_grad, key_weight, adapter_down, adapter_up, segment_adapter, adapter_slot, live_segments):
     args = (layer_input, output_grad, key_weight, adapter_down, adapter_up, segment_adapter, adapter_slot, live_segments)
     seg_group = segment_adapter.shape[0] // lax.axis_size("dp")
-    one_each = seg_group == lax.axis_size("tensor")
+    one_each = seg_group == lax.axis_size("tensor") == 8
     tiled = adapter_up.shape[2] % 128 == 0 and layer_input.shape[1] % 256 == 0
     if one_each and tiled and lax.axis_size("dp") % 2 == 0:
         return fused(*args)

time: 45.9 us -> 42.2 us (0.919)
  Pallas kernels: 44.5 us -> 40.8 us
    pallas_call x1, Pallas kernels: 41.6 us -> 37.9 us  [fused(): pl.pallas_call(functools.partial(fused_kernel, dims), out_shape=(jax.Shap...]
where the time goes in v2:
time: 42.2 us; the launch traced here: 42.1 us
  Pallas kernels  40.8 us (97%)
  between operations  1.29 us (3%)
    pallas_call x1, Pallas kernels, fused(): pl.pallas_call(functools.partial(fused_kernel, dims), out_shape=(jax.Shap...  37.9 us
    pallas_call x1, Pallas kernels, fused(): pl.pallas_call(store_kernel, out_shape=tuple((jax.ShapeDtypeStruct(r.shap...  2.85 us

profile of v2, /device:TPU:0, one launch (start us, length us, event | category | flops | bytes accessed | tf_op | source)
XLA Modules:
  0.0 42.1 jit_solution(12292315269121012057)
XLA Ops:
  1.3 37.9 %shard_map.103 = (bf16[8,128,1024]{2,1,0:T(8,128)(2,1)}, bf16[32,16,1024]{2,1,0:T(8,128)(2,1)}, bf16[32,16,128]{2,1,0:T(8,128)(2,1)}) custom-call(s32[32]{0:T(128)} %adapter_hbm.1, s32[128]{0:T(128)} %slot_hbm.1, s32[1]{0:T(128)S(6)} %copy.11.live_hbm, bf16[8,128,1024]{2,1,0:T(8,128)(2,1)} %bitcast.2, bf16[128,1024]{1,0:T(8,128)(2,1)} %og_hbm.1, ...), custom_call_target="tpu_custom_call" | custom-call | flops 2281701376 | bytes 8388608 | tf_op jit(solution)/shard_map/pallas_call | solution.py:430
  39.2 2.9 %shard_map.104 = (bf16[8,128,1024]{2,1,0:T(8,128)(2,1)}, bf16[32,16,1024]{2,1,0:T(8,128)(2,1)}, bf16[32,16,128]{2,1,0:T(8,128)(2,1)}) custom-call(bf16[8,128,1024]{2,1,0:T(8,128)(2,1)} %get-tuple-element.9.a, bf16[32,16,1024]{2,1,0:T(8,128)(2,1)} %get-tuple-element.10.b, bf16[32,16,128]{2,1,0:T(8,128)(2,1)} %get-tuple-element.11.c), custom_call_target="tpu_custom_call" | custom-call | bytes 6291456 | tf_op jit(solution)/shard_map/pallas_call | solution.py:467

commit v3 on v2

--- a/solution.py
+++ b/solution.py
@@ -68,9 +68,6 @@
         pltpu.make_async_copy(x_hbm, x_v, load_sem.at[3]),
         pltpu.make_async_copy(kw_hbm, kw_v, load_sem.at[4]),
     ]
-    for copy in scalars + loads:
-        copy.start()
-
     tensor_peers = [lax.rem(t + j, T) for j in range(1, T)]
     far = [lax.rem(y + j, Y) for j in range(1, Y)]
     barrier = pltpu.get_barrier_semaphore()
@@ -79,6 +76,9 @@
     dp_peers = [lax.rem(q + j, Q) for j in range(1, Q)]
     for peer in dp_peers:
         pl.semaphore_signal(barrier, inc=1, device_id={"dp": peer}, device_id_type=MESH)
+
+    for copy in scalars[2:] + loads[:1] + scalars[:2] + loads[1:]:
+        copy.start()
 
     scalars[2].wait()
     loads[0].wait()
@@ -158,6 +158,8 @@
         return carry
 
     lax.fori_loop(0, Y * S, choose_down, 0)
+    send(s1d_out, s1d_in, s1_send.at[0], s1_recv.at[0], {"dp": mate})
+
     loads[1].wait()
 
     def choose_up(i, carry):
@@ -169,38 +171,13 @@
     lax.fori_loop(0, Q * S, choose_up, 0)
     for copy in later_loads:
         copy.start()
-    send(s1d_out, s1d_in, s1_send.at[0], s1_recv.at[0], {"dp": mate})
-
     for peer in dp_peers:
         send(fu_out.at[peer], fu_in.at[q], fu_send.at[peer], fu_recv.at[q], {"dp": peer})
     start_own(2)
     start_own(3)
 
-    def first_of(p, carry):
-        slot = q * PO + p
-        for group in range(Q):
-            index = jnp.int32(-1)
-            for s in reversed(range(S)):
-                index = jnp.where(seg_slot[group * S + s] == slot, jnp.int32(s), index)
-            first[p * Q + group] = index
-        return carry
-
-    lax.fori_loop(0, PO, first_of, 0)
-
-    arrived(s1d_in, s1_recv.at[0])
-    part_segs = S // 2
-
-    def segs(piece):
-        return pl.ds(piece * part_segs, part_segs)
-
-    for piece in range(2):
-        def combine_piece(i, carry):
-            return combine_down(i // part_segs * S + piece * part_segs + lax.rem(i, part_segs), carry)
-
-        lax.fori_loop(0, Y * part_segs, combine_piece, 0)
-        for other in far:
-            send(s2d_out.at[other, segs(piece)], s2d_in.at[y, segs(piece)], s2_send.at[other, piece],
-                 s2_recv.at[y, piece], {"dp": other * 2 + c})
+    forward(1, 0)
+
     total = fu_out[q]
     for peer in dp_peers:
         arrived(fu_in.at[peer], fu_recv.at[peer])
@@ -210,7 +187,23 @@
         send(up_seg.at[peer], up_own.at[t], up_send.at[peer], up_recv.at[t], {"tensor": peer})
     up_own[t] = up_seg[t]
 
-    forward(1, 0)
+    arrived(s1d_in, s1_recv.at[0])
+    part_segs = S // 2
+
+    def segs(piece):
+        return pl.ds(piece * part_segs, part_segs)
+
+    for piece in range(2):
+        def combine_piece(i, carry):
+            return combine_down(i // part_segs * S + piece * part_segs + lax.rem(i, part_segs), carry)
+
+        lax.fori_loop(0, Y * part_segs, combine_piece, 0)
+        for other in far:
+            send(s2d_out.at[other, segs(piece)], s2d_in.at[y, segs(piece)], s2_send.at[other, piece],
+                 s2_recv.at[y, piece], {"dp": other * 2 + c})
+
+    forward(1, 1)
+    forward(1, 2)
 
     for peer in tensor_peers:
         arrived(up_own.at[peer], up_recv.at[peer])
@@ -223,10 +216,9 @@
     for peer in tensor_peers:
         send(lr.at[t], lr.at[t], lr_send.at[peer], lr_recv.at[t], {"tensor": peer})
 
-    forward(1, 1)
-    forward(1, 2)
-
-    later_loads[0].wait()
+    forward(1, 3)
+    forward(2, 0)
+
 
     def down_of(s, carry):
         rows = s2d_out[y, s]
@@ -248,8 +240,7 @@
             def _():
                 pr_in[t] = pr_out[s]
 
-    project(0)
-    forward(1, 3)
+    later_loads[0].wait()
 
     for peer in tensor_peers:
         arrived(lr.at[peer], lr_recv.at[peer])
@@ -275,10 +266,12 @@
              {"dp": other * 2 + c})
     send(rows_d.at[q], rows_d.at[q], rwc_send.at[q], rw_recv.at[q, 0], {"dp": mate})
 
-    forward(2, 0)
+    forward(2, 1)
+    project(0)
+    forward(2, 2)
     project(1)
-    forward(2, 1)
-    later_loads[1].wait()
+    forward(2, 3)
+
 
     def two_blocks(pair):
         left_rows = jnp.concatenate([whole[origin] for origin in pair], axis=0)
@@ -302,8 +295,11 @@
     other = lax.rem(x + 1, X)
 
     wait_side(column, range(CHUNKS))
+    for part in range(direct, CHUNKS):
+        share(part)
+    forward(3, 0)
+    later_loads[1].wait()
     two_blocks((t, column))
-    forward(2, 2)
 
     for peer in tensor_peers:
         arrived(pr_in.at[peer], pr_recv.at[peer])
@@ -319,12 +315,18 @@
         send(su_out.at[peer], su_in.at[t], su_send.at[peer], su_recv.at[t], {"tensor": peer})
     su_in[t] = su_out[t]
 
-    forward(2, 3)
-    for part in range(direct, CHUNKS):
-        share(part)
-    forward(3, 0)
-    two_blocks((pair_z * X + x, near_row * X + x))
     forward(3, 1)
+
+    def first_of(p, carry):
+        slot = q * PO + p
+        for group in range(Q):
+            index = jnp.int32(-1)
+            for s in reversed(range(S)):
+                index = jnp.where(seg_slot[group * S + s] == slot, jnp.int32(s), index)
+            first[p * Q + group] = index
+        return carry
+
+    lax.fori_loop(0, PO, first_of, 0)
 
     for peer in tensor_peers:
         arrived(su_in.at[peer], su_recv.at[peer])
@@ -337,13 +339,17 @@
     for peer in dp_peers:
         send(rows_u.at[q], rows_u.at[q], rwu_send.at[peer], rw_recv.at[q, 1], {"dp": peer})
 
+    settled = list(pending)
+    pending.clear()
     forward(3, 2)
+    forward(3, 3)
+    two_blocks((pair_z * X + x, near_row * X + x))
+
     for far_chip in far:
         origin = far_chip * 2 + c
         arrived(rows_d.at[origin], rw_recv.at[origin, 0])
         send(rows_d.at[origin], rows_d.at[origin], rwc_send.at[origin],
              rw_recv.at[origin, 0], {"dp": mate})
-    forward(3, 3)
     wait_side(near_row * X + other, range(CHUNKS))
     two_blocks((far_row * X + x, near_row * X + other))
 
@@ -374,20 +380,24 @@
     ]
     stores[0].start()
 
-    wait_side(far_row * X + other, range(CHUNKS))
-    wait_side(pair_z * X + other, range(CHUNKS))
-    two_blocks((pair_z * X + other, far_row * X + other))
-
     for peer in dp_peers:
         arrived(rows_u.at[peer], rw_recv.at[peer, 1])
     lax.fori_loop(0, PO, owner_up, 0, unroll=4)
     stores[1].start()
 
-    for when, copy in pending:
-        if when is None:
-            copy.wait_send()
-        else:
-            pl.when(when)(copy.wait_send)
+    def settle(sends):
+        for when, copy in sends:
+            if when is None:
+                copy.wait_send()
+            else:
+                pl.when(when)(copy.wait_send)
+
+    settle(settled)
+    wait_side(far_row * X + other, range(CHUNKS))
+    wait_side(pair_z * X + other, range(CHUNKS))
+    two_blocks((pair_z * X + other, far_row * X + other))
+
+    settle(pending)
     for origin in range(T):
         pltpu.make_async_copy(ig_v.at[origin], ig_hbm.at[origin], store_sem.at[origin]).wait()
     for copy in stores:

time: 42.2 us -> 44.5 us (1.055)
  Pallas kernels: 40.8 us -> 43.1 us
    pallas_call x1, Pallas kernels: 37.9 us -> 40.2 us  [fused(): pl.pallas_call(functools.partial(fused_kernel, dims), out_shape=(jax.Shap...]
where the time goes in v3:
time: 44.5 us; the launch traced here: 44.3 us
  Pallas kernels  43.1 us (97%)
  between operations  1.29 us (3%)
    pallas_call x1, Pallas kernels, fused(): pl.pallas_call(functools.partial(fused_kernel, dims), out_shape=(jax.Shap...  40.2 us
    pallas_call x1, Pallas kernels, fused(): pl.pallas_call(store_kernel, out_shape=tuple((jax.ShapeDtypeStruct(r.shap...  2.85 us

profile of v3, /device:TPU:0, one launch (start us, length us, event | category | flops | bytes accessed | tf_op | source)
XLA Modules:
  0.0 44.3 jit_solution(1220978811427727328)
XLA Ops:
  1.3 40.2 %shard_map.103 = (bf16[8,128,1024]{2,1,0:T(8,128)(2,1)}, bf16[32,16,1024]{2,1,0:T(8,128)(2,1)}, bf16[32,16,128]{2,1,0:T(8,128)(2,1)}) custom-call(s32[32]{0:T(128)} %adapter_hbm.1, s32[128]{0:T(128)} %slot_hbm.1, s32[1]{0:T(128)S(6)} %copy.11.live_hbm, bf16[8,128,1024]{2,1,0:T(8,128)(2,1)} %bitcast.2, bf16[128,1024]{1,0:T(8,128)(2,1)} %og_hbm.1, ...), custom_call_target="tpu_custom_call" | custom-call | flops 2281701376 | bytes 8388608 | tf_op jit(solution)/shard_map/pallas_call | solution.py:440
  41.5 2.9 %shard_map.104 = (bf16[8,128,1024]{2,1,0:T(8,128)(2,1)}, bf16[32,16,1024]{2,1,0:T(8,128)(2,1)}, bf16[32,16,128]{2,1,0:T(8,128)(2,1)}) custom-call(bf16[8,128,1024]{2,1,0:T(8,128)(2,1)} %get-tuple-element.9.a, bf16[32,16,1024]{2,1,0:T(8,128)(2,1)} %get-tuple-element.10.b, bf16[32,16,128]{2,1,0:T(8,128)(2,1)} %get-tuple-element.11.c), custom_call_target="tpu_custom_call" | custom-call | bytes 6291456 | tf_op jit(solution)/shard_map/pallas_call | solution.py:477

commit v4 on v2

--- a/solution.py
+++ b/solution.py
@@ -68,9 +68,6 @@
         pltpu.make_async_copy(x_hbm, x_v, load_sem.at[3]),
         pltpu.make_async_copy(kw_hbm, kw_v, load_sem.at[4]),
     ]
-    for copy in scalars + loads:
-        copy.start()
-
     tensor_peers = [lax.rem(t + j, T) for j in range(1, T)]
     far = [lax.rem(y + j, Y) for j in range(1, Y)]
     barrier = pltpu.get_barrier_semaphore()
@@ -79,6 +76,9 @@
     dp_peers = [lax.rem(q + j, Q) for j in range(1, Q)]
     for peer in dp_peers:
         pl.semaphore_signal(barrier, inc=1, device_id={"dp": peer}, device_id_type=MESH)
+
+    for copy in scalars[2:] + loads[:1] + scalars[:2] + [loads[2], loads[1]]:
+        copy.start()
 
     scalars[2].wait()
     loads[0].wait()
@@ -158,6 +158,8 @@
         return carry
 
     lax.fori_loop(0, Y * S, choose_down, 0)
+    send(s1d_out, s1d_in, s1_send.at[0], s1_recv.at[0], {"dp": mate})
+
     loads[1].wait()
 
     def choose_up(i, carry):
@@ -169,8 +171,6 @@
     lax.fori_loop(0, Q * S, choose_up, 0)
     for copy in later_loads:
         copy.start()
-    send(s1d_out, s1d_in, s1_send.at[0], s1_recv.at[0], {"dp": mate})
-
     for peer in dp_peers:
         send(fu_out.at[peer], fu_in.at[q], fu_send.at[peer], fu_recv.at[q], {"dp": peer})
     start_own(2)
@@ -337,6 +337,8 @@
     for peer in dp_peers:
         send(rows_u.at[q], rows_u.at[q], rwu_send.at[peer], rw_recv.at[q, 1], {"dp": peer})
 
+    settled = list(pending)
+    pending.clear()
     forward(3, 2)
     for far_chip in far:
         origin = far_chip * 2 + c
@@ -374,20 +376,25 @@
     ]
     stores[0].start()
 
-    wait_side(far_row * X + other, range(CHUNKS))
-    wait_side(pair_z * X + other, range(CHUNKS))
-    two_blocks((pair_z * X + other, far_row * X + other))
 
     for peer in dp_peers:
         arrived(rows_u.at[peer], rw_recv.at[peer, 1])
     lax.fori_loop(0, PO, owner_up, 0, unroll=4)
     stores[1].start()
 
-    for when, copy in pending:
-        if when is None:
-            copy.wait_send()
-        else:
-            pl.when(when)(copy.wait_send)
+    def settle(sends):
+        for when, copy in sends:
+            if when is None:
+                copy.wait_send()
+            else:
+                pl.when(when)(copy.wait_send)
+
+    settle(settled)
+    wait_side(far_row * X + other, range(CHUNKS))
+    wait_side(pair_z * X + other, range(CHUNKS))
+    two_blocks((pair_z * X + other, far_row * X + other))
+
+    settle(pending)
     for origin in range(T):
         pltpu.make_async_copy(ig_v.at[origin], ig_hbm.at[origin], store_sem.at[origin]).wait()
     for copy in stores:

time: 42.2 us -> 42 us (level)
  no operation moved by 1% of the time
where the time goes in v4:
time: 42 us; the launch traced here: 41.8 us
  Pallas kernels  40.6 us (97%)
  between operations  1.29 us (3%)
    pallas_call x1, Pallas kernels, fused(): pl.pallas_call(functools.partial(fused_kernel, dims), out_shape=(jax.Shap...  37.7 us
    pallas_call x1, Pallas kernels, fused(): pl.pallas_call(store_kernel, out_shape=tuple((jax.ShapeDtypeStruct(r.shap...  2.85 us

profile of v4, /device:TPU:0, one launch (start us, length us, event | category | flops | bytes accessed | tf_op | source)
XLA Modules:
  0.0 41.8 jit_solution(15935852388942831790)
XLA Ops:
  1.3 37.7 %shard_map.103 = (bf16[8,128,1024]{2,1,0:T(8,128)(2,1)}, bf16[32,16,1024]{2,1,0:T(8,128)(2,1)}, bf16[32,16,128]{2,1,0:T(8,128)(2,1)}) custom-call(s32[32]{0:T(128)} %adapter_hbm.1, s32[128]{0:T(128)} %slot_hbm.1, s32[1]{0:T(128)S(6)} %copy.11.live_hbm, bf16[8,128,1024]{2,1,0:T(8,128)(2,1)} %bitcast.2, bf16[128,1024]{1,0:T(8,128)(2,1)} %og_hbm.1, ...), custom_call_target="tpu_custom_call" | custom-call | flops 2281701376 | bytes 8388608 | tf_op jit(solution)/shard_map/pallas_call | solution.py:437
  39.0 2.9 %shard_map.104 = (bf16[8,128,1024]{2,1,0:T(8,128)(2,1)}, bf16[32,16,1024]{2,1,0:T(8,128)(2,1)}, bf16[32,16,128]{2,1,0:T(8,128)(2,1)}) custom-call(bf16[8,128,1024]{2,1,0:T(8,128)(2,1)} %get-tuple-element.9.a, bf16[32,16,1024]{2,1,0:T(8,128)(2,1)} %get-tuple-element.10.b, bf16[32,16,128]{2,1,0:T(8,128)(2,1)} %get-tuple-element.11.c), custom_call_target="tpu_custom_call" | custom-call | bytes 6291456 | tf_op jit(solution)/shard_map/pallas_call | solution.py:474
